TPU v7x, 512 devices: a whole 4x8x8 slice. The times are simulated.
512 devices in a mesh: list: 16 (over z, core), sub: 8 (over y), slab: 4 (over x).
Axes of the slice: x: 4, y: 8, z: 8, core: 2. Of those that a mesh axis runs over, the one named last changes fastest.
Arguments:
- vectors: float32 [1024, 65536], P(None, ('list', 'sub', 'slab')), may hold values from -10 to 10
- centroids: bfloat16 [1024, 262144], P('sub', ('list', 'slab')), may hold values from -3 to 3
- codebook: float32 [32, 256, 32], P('sub'), may hold values from -10 to 10
- list_ids: int32 [65536], P(('list', 'sub', 'slab')), may hold values from 0 to 262143, as said below
Outputs:
- fresh_codebook: float32 [32, 256, 32], P('sub')
Inputs may be any that keep to these rules, and one draw needn't show every extreme that they name: `list_ids`: among the columns of one device, at most 4 name lists of one owner (list id // 4096); in every draw one owner receives exactly 4 from every device.
All inputs are finite; a program needn't handle non-finite values.
Results may differ from a plain program's by a relative error of at most 0.0003.
Values sent between devices are 32-bit elements; how exact they have to be, the bound alone decides.
A program may use at most 64 MiB of HBM per device.

v0:
```python
import math

import jax
import jax.numpy as jnp
from jax import lax
from jax.sharding import PartitionSpec as P

SOFTMAX_HEAT = 8.0
PRIOR_MASS = 1.0


def owner_rank(owner_of, owners):
    row_count = owner_of.shape[0]
    matches = (owner_of[:, None] == jnp.arange(owners)[None, :]).astype(jnp.float32)
    block = math.gcd(row_count, 128)
    blocks = matches.reshape(row_count // block, block, owners)
    strict_lower = (jnp.arange(block)[:, None] > jnp.arange(block)[None, :]).astype(jnp.float32)
    inside = jnp.einsum("ij,bjo->bio", strict_lower, blocks)
    totals = jnp.sum(blocks, axis=1)
    before = jnp.cumsum(totals, axis=0) - totals
    ranking = (inside + before[:, None, :]).reshape(row_count, owners)
    return jnp.sum(ranking * matches, axis=1).astype(jnp.int32)


def soft_sums(residual, weight, codebook):
    groups, num_codes, width = codebook.shape
    total_columns = residual.shape[1]
    block = math.gcd(total_columns, 1024)
    codeword_norm = jnp.sum(codebook * codebook, axis=-1)

    def block_step(loop_index, running):
        counts, weighted = running
        offset = (loop_index * block).astype(jnp.int32)
        column_piece = lax.dynamic_slice_in_dim(residual, offset, block, 1).reshape(
            groups, width, block
        )
        present = lax.dynamic_slice_in_dim(weight, offset, block, 0)
        inner_products = jnp.einsum(
            "skd,sdn->skn", codebook, column_piece, precision=lax.Precision.HIGHEST
        )
        assignment_scores = (2.0 * inner_products - codeword_norm[:, :, None]) / SOFTMAX_HEAT
        assignment_scores = assignment_scores - jnp.max(assignment_scores, axis=1, keepdims=True)
        exponent = jnp.exp(assignment_scores)
        assign = exponent / jnp.sum(exponent, axis=1, keepdims=True) * present[None, None, :]
        counts = counts + jnp.sum(assign, axis=2)
        weighted = weighted + jnp.einsum(
            "skn,sdn->skd", assign, column_piece, precision=lax.Precision.HIGHEST
        )
        return (counts, weighted)

    start_state = (
        jnp.zeros((groups, num_codes), jnp.float32),
        jnp.zeros((groups, num_codes, width), jnp.float32),
    )
    return lax.fori_loop(0, total_columns // block, block_step, start_state)


def refresh(counts, weighted, previous):
    return (weighted + PRIOR_MASS * previous) / (counts[:, :, None] + PRIOR_MASS)


def per_device(vectors, centroids, codebook, list_ids):
    list_count = lax.axis_size("list")
    slab_count = lax.axis_size("slab")
    sub_count = lax.axis_size("sub")
    owners = list_count * slab_count
    lists_here = centroids.shape[1]
    row_count = vectors.shape[1]
    capacity = 2 * row_count // owners
    owner_of = list_ids // lists_here
    within = (list_ids % lists_here).astype(jnp.float32)
    slot = owner_of * capacity + owner_rank(owner_of, owners)
    packed = jnp.zeros((vectors.shape[0], owners * capacity), jnp.float32).at[:, slot].set(vectors)
    labels = jnp.full((owners * capacity,), -1.0, jnp.float32).at[slot].set(within)
    labels = jnp.broadcast_to(labels[None, :], (sub_count, owners * capacity))
    arrived, arrived_labels = (
        lax.all_to_all(packed, ("list", "slab"), split_axis=1, concat_axis=1, tiled=True),
        lax.all_to_all(labels, ("list", "slab"), split_axis=1, concat_axis=1, tiled=True),
    )
    columns, column_labels = (
        lax.all_to_all(arrived, "sub", split_axis=0, concat_axis=1, tiled=True),
        lax.all_to_all(arrived_labels, "sub", split_axis=0, concat_axis=1, tiled=True),
    )
    final_labels = column_labels[0]
    present = final_labels >= 0.0
    weight = present.astype(jnp.float32)
    list_index = jnp.where(present, final_labels, 0.0).astype(jnp.int32)
    nearest = jnp.take(centroids, list_index, axis=1).astype(jnp.float32)
    residual = (columns - nearest) * weight[None, :]
    counts, weighted = soft_sums(residual, weight, codebook)
    counts, weighted = lax.psum((counts, weighted), ("list", "slab"))
    return refresh(counts, weighted, codebook)


def solution(mesh):
    return jax.shard_map(
        per_device,
        mesh=mesh,
        in_specs=(
            P(None, ("list", "sub", "slab")),
            P("sub", ("list", "slab")),
            P("sub", None, None),
            P(("list", "sub", "slab")),
        ),
        out_specs=P("sub", None, None),
        check_vma=False,
    )
```

profile of v0, /device:TPU:1, one launch (start us, length us, event | category | flops | bytes accessed | tf_op | source)
XLA Modules:
  0.0 453.4 jit_solution(12421118974912579844)
XLA Ops:
  6.5 0.7 fusion.23
  7.5 1.0 scatter_custom_fusion.1
  8.6 0.8 broadcast_in_dim.61
  9.4 14.8 %all-to-all-start.2 = ((f32[8,64,4]{0,2,1:T(4,128)}), f32[8,64,4]{0,2,1:T(4,128)S(1)}, u32[]{:S(2)}, u32[]{:S(2)}) async-start(f32[8,64,4]{0,2,1:T(4,128)} %broadcast_in_dim.61), calls=%async_computation.2 | async-start | bytes 262144 | tf_op jit(solution)/shard_map/all_to_all | solution.py:78
  24.2 1.2 copy.24
  25.5 1.3 scatter_custom_fusion
  26.8 1.3 all_to_all.34
  28.1 6.1 %all-to-all-done.2 = f32[8,64,4]{0,2,1:T(4,128)S(1)} async-done(((f32[8,64,4]{0,2,1:T(4,128)}), f32[8,64,4]{0,2,1:T(4,128)S(1)}, u32[]{:S(2)}, u32[]{:S(2)}) %all-to-all-start.2) | async-done | bytes 8224 | tf_op jit(solution)/shard_map/all_to_all | solution.py:78
  34.2 6.0 %all-to-all-start = ((f32[1024,64,4]{0,2,1:T(4,128)}), f32[1024,64,4]{0,2,1:T(4,128)S(1)}, u32[]{:S(2)}, u32[]{:S(2)}) async-start(f32[1024,64,4]{0,2,1:T(4,128)} %all_to_all.34), calls=%async_computation | async-start | bytes 2097152 | tf_op jit(solution)/shard_map/all_to_all | solution.py:77
  40.2 0.7 copy.26
  40.8 27.1 %all-to-all-done = f32[1024,64,4]{0,2,1:T(4,128)S(1)} async-done(((f32[1024,64,4]{0,2,1:T(4,128)}), f32[1024,64,4]{0,2,1:T(4,128)S(1)}, u32[]{:S(2)}, u32[]{:S(2)}) %all-to-all-start) | async-done | bytes 1048608 | tf_op jit(solution)/shard_map/all_to_all | solution.py:77
  68.0 6.8 %all-to-all-start.3 = ((f32[8,1,256]{2,1,0:T(1,128)}), f32[8,1,256]{2,1,0:T(1,128)S(1)}, u32[]{:S(2)}, u32[]{:S(2)}) async-start(f32[8,1,256]{2,1,0:T(1,128)} %copy.26), calls=%async_computation.3 | async-start | bytes 16384 | tf_op jit(solution)/shard_map/all_to_all | solution.py:82
  74.8 0.4 all_to_all.36
  75.2 1.2 copy.25
  76.4 5.0 %all-to-all-done.3 = f32[8,1,256]{2,1,0:T(1,128)S(1)} async-done(((f32[8,1,256]{2,1,0:T(1,128)}), f32[8,1,256]{2,1,0:T(1,128)S(1)}, u32[]{:S(2)}, u32[]{:S(2)}) %all-to-all-start.3) | async-done | bytes 8224 | tf_op jit(solution)/shard_map/all_to_all | solution.py:82
  81.4 3.6 all-to-all-start.1
  85.2 0.7 copy.27
  85.9 6.2 %gather_fusion = bf16[2048,128]{1,0:T(8,128)(2,1)S(1)} fusion(bf16[128,4096]{0,1:T(8,128)(2,1)S(1)} %copy.27, s32[2048]{0:T(1024)S(1)} %broadcast_clamp_fusion), kind=kCustom, calls=%fused_computation | custom fusion | bytes 1056768 | tf_op jit(solution)/shard_map/jit(_take)/gather | solution.py:88
  92.1 19.6 %all-to-all-done.1 = f32[8,128,256]{1,2,0:T(8,128)S(1)} async-done(((f32[8,128,256]{1,2,0:T(8,128)}), f32[8,128,256]{1,2,0:T(8,128)S(1)}, u32[]{:S(2)}, u32[]{:S(2)}) %all-to-all-start.1) | async-done | bytes 1048608 | tf_op jit(solution)/shard_map/all_to_all | solution.py:81
  111.7 0.8 fusion.17
  112.5 27.6 %while.16 = (s32[]{:T(128)}, f32[4,256]{1,0:T(4,128)S(1)}, f32[4,256,32]{1,2,0:T(8,128)S(1)}, f32[128,2048]{0,1:T(8,128)S(1)}, f32[4,256,32]{1,2,0:T(8,128)S(1)}...) while((s32[]{:T(128)}, f32[4,256]{1,0:T(4,128)S(1)}, ...), condition=%wide.region_9.10_spmd.clone, body=%wide.region_5.9_spmd.clone.sunk | while | flops 819004672 | bytes 41373896 | solution.py:55
  112.8 3.5 fusion.41
  116.2 3.0 fusion.42
  119.2 6.5 %fusion.44 = f32[4,256,32]{1,2,0:T(8,128)S(1)} fusion(f32[4,32,1024]{2,1,0:T(8,128)S(1)} %bitcast.61, f32[4,256,1024]{2,1,0:T(8,128)} %get-tuple-element.256, f32[1024]{0:T(1024)S(1)} %dynamic_slice.20, f32[4,1024]{1,0:T(4,128)S(1)} %get-tuple-element.257, f32[4,256,32]{1,2,0:T(8,128)S(1)} %get-tuple-element.271, pred[]{:T(512)S(6)} %compare.6), kind=kOutput, calls=%fused_computation.15.clone.1 | convolution fusion | flops 404815872 | bytes 5001217 | tf_op jit(solution)/shard_map/while/body/eval_jaxpr/skn,sdn->skd/dot_general | solution.py:46
  125.8 0.5 fusion.43
  126.6 3.5 fusion.41
  130.0 3.0 fusion.42
  133.0 6.5 %fusion.44 = f32[4,256,32]{1,2,0:T(8,128)S(1)} fusion(f32[4,32,1024]{2,1,0:T(8,128)S(1)} %bitcast.61, f32[4,256,1024]{2,1,0:T(8,128)} %get-tuple-element.256, f32[1024]{0:T(1024)S(1)} %dynamic_slice.20, f32[4,1024]{1,0:T(4,128)S(1)} %get-tuple-element.257, f32[4,256,32]{1,2,0:T(8,128)S(1)} %get-tuple-element.271, pred[]{:T(512)S(6)} %compare.6), kind=kOutput, calls=%fused_computation.15.clone.1 | convolution fusion | flops 404815872 | bytes 5001217 | tf_op jit(solution)/shard_map/while/body/eval_jaxpr/skn,sdn->skd/dot_general | solution.py:46
  139.6 0.5 fusion.43
  140.1 123.2 %psum.15 = f32[4,256]{1,0:T(4,128)S(1)} all-reduce(f32[4,256]{1,0:T(4,128)S(1)} %get-tuple-element.131), channel_id=1, replica_groups=mesh['list'=16,'sub'=8,'slab'=4] {'list','slab'}, use_global_device_ids=true, to_apply=%region_11.12 | all-reduce | flops 1024 | bytes 8192 | tf_op jit(solution)/shard_map/psum | solution.py:91
  263.4 181.7 %all-reduce.2.cloned.1.call-done = f32[4,256,32]{1,2,0:T(8,128)} async-done(((f32[4,256,32]{1,2,0:T(8,128)}), f32[4,256,32]{1,2,0:T(8,128)}) %all-reduce.2.cloned.1.call-update) | async-done | bytes 131088 | tf_op jit(solution)/shard_map/psum | solution.py:91
  445.0 1.6 add_divide_fusion
  (32 shorter events, 1.2 us)
Async XLA Ops:
  9.4 24.8 %all-to-all-start.2 = ((f32[8,64,4]{0,2,1:T(4,128)}), f32[8,64,4]{0,2,1:T(4,128)S(1)}, u32[]{:S(2)}, u32[]{:S(2)}) async-start(f32[8,64,4]{0,2,1:T(4,128)} %broadcast_in_dim.61), calls=%async_computation.2 | async-start | bytes 262144 | tf_op jit(solution)/shard_map/all_to_all | solution.py:78
  28.1 57.1 %copy-start.2 = (bf16[128,4096]{1,0:T(8,128)(2,1)S(1)}, bf16[128,4096]{1,0:T(8,128)(2,1)}, u32[]{:S(2)}) copy-start(bf16[128,4096]{1,0:T(8,128)(2,1)} %param.7) | copy-start | bytes 3145732
  34.2 33.8 %all-to-all-start = ((f32[1024,64,4]{0,2,1:T(4,128)}), f32[1024,64,4]{0,2,1:T(4,128)S(1)}, u32[]{:S(2)}, u32[]{:S(2)}) async-start(f32[1024,64,4]{0,2,1:T(4,128)} %all_to_all.34), calls=%async_computation | async-start | bytes 2097152 | tf_op jit(solution)/shard_map/all_to_all | solution.py:77
  68.0 13.4 %all-to-all-start.3 = ((f32[8,1,256]{2,1,0:T(1,128)}), f32[8,1,256]{2,1,0:T(1,128)S(1)}, u32[]{:S(2)}, u32[]{:S(2)}) async-start(f32[8,1,256]{2,1,0:T(1,128)} %copy.26), calls=%async_computation.3 | async-start | bytes 16384 | tf_op jit(solution)/shard_map/all_to_all | solution.py:82
  74.8 11.1 %copy-start.1 = (f32[4,256,32]{1,2,0:T(8,128)S(1)}, f32[4,256,32]{1,2,0:T(8,128)}, u32[]{:S(2)}) copy-start(f32[4,256,32]{1,2,0:T(8,128)} %param.8) | copy-start | bytes 393220
  81.4 30.4 %all-to-all-start.1 = ((f32[8,128,256]{1,2,0:T(8,128)}), f32[8,128,256]{1,2,0:T(8,128)S(1)}, u32[]{:S(2)}, u32[]{:S(2)}) async-start(f32[8,128,256]{1,2,0:T(8,128)} %copy.25), calls=%async_computation.1 | async-start | bytes 2097152 | tf_op jit(solution)/shard_map/all_to_all | solution.py:81
  84.9 360.1 %all-reduce.2.cloned.1.call-start = ((), (), s32[]{:S(2)}) async-start(), calls=%async_computation.4 | async-start | bytes 262144 | tf_op jit(solution)/shard_map/psum | solution.py:91
  119.2 6.5 %copy-start = (f32[4,256,1024]{2,1,0:T(8,128)S(1)}, f32[4,256,1024]{2,1,0:T(8,128)}, u32[]{:S(2)}) copy-start(f32[4,256,1024]{2,1,0:T(8,128)} %get-tuple-element.256) | copy-start | bytes 12582916 | tf_op jit(solution)/shard_map/while
  133.0 6.5 %copy-start = (f32[4,256,1024]{2,1,0:T(8,128)S(1)}, f32[4,256,1024]{2,1,0:T(8,128)}, u32[]{:S(2)}) copy-start(f32[4,256,1024]{2,1,0:T(8,128)} %get-tuple-element.256) | copy-start | bytes 12582916 | tf_op jit(solution)/shard_map/while
  140.1 123.2 %copy-start.3 = (f32[4,256,32]{1,2,0:T(8,128)}, f32[4,256,32]{1,2,0:T(8,128)S(1)}, u32[]{:S(2)}) copy-start(f32[4,256,32]{1,2,0:T(8,128)S(1)} %get-tuple-element.130) | copy-start | bytes 393220
Sparse Core Ops, SparseCore 0:
  263.5 181.4 all-reduce.1
where the time goes:
time: 454 us; the launch traced here: 453 us
  waiting for transfers between devices  239 us (53%)
  blocking collectives  123 us (27%)
  starting transfers between devices  31.4 us (7%)
  matrix products  20.1 us (4%)
  local copies, waits for them, and re-layouts  15.3 us (3%)
  between operations  13.6 us (3%)
  other arithmetic  10.2 us (2%)
    psum x1, waiting for transfers between devices, per_device(): counts, weighted = lax.psum((counts, weighted), ('list', 'slab'))  182 us
    psum x1, blocking collectives, per_device(): counts, weighted = lax.psum((counts, weighted), ('list', 'slab'))  123 us
    all_to_all x1, waiting for transfers between devices, per_device(): lax.all_to_all(packed, ('list', 'slab'), split_axis=1, concat_axis=1, til...  27.1 us
    all_to_all x1, waiting for transfers between devices, per_device(): lax.all_to_all(arrived, 'sub', split_axis=0, concat_axis=1, tiled=True)  19.6 us
    all_to_all x1, starting transfers between devices, per_device(): lax.all_to_all(labels, ('list', 'slab'), split_axis=1, concat_axis=1, til...  14.8 us
    dot_general x2, matrix products, block_step(): jnp.einsum('skn,sdn->skd', assign, column_piece, precision=lax.Precision....  13 us
  transfers between devices with their start and end apart: 5, of which 5 were waited for; matrix products, arithmetic and copies ran while one was open for 2% of the time, Pallas kernels for 0%

commit v1 on v0

v1 whole, which is shorter than its diff:
```python
import functools
import math

import jax
import jax.numpy as jnp
from jax import lax
from jax.experimental import pallas as pl
from jax.experimental.pallas import tpu as pltpu
from jax.sharding import PartitionSpec as P

SOFTMAX_HEAT = 8.0
PRIOR_MASS = 1.0
MESH = pl.DeviceIdType.MESH
F32, BF16, I32 = jnp.float32, jnp.bfloat16, jnp.int32
CAP = 4


def split3(x):
    a = x.astype(BF16)
    rest = x - a.astype(F32)
    b = rest.astype(BF16)
    c = (rest - b.astype(F32)).astype(BF16)
    return a, b, c


def dot(a, b, ca=1, cb=0):
    return lax.dot_general(a, b, (((ca,), (cb,)), ((), ())), preferred_element_type=F32)


def iota(shape, dim):
    return lax.broadcasted_iota(I32, shape, dim)


def kernel(
    dims,
    ids_ref, vec_ref, cen_ref, cb_ref,
    out_ref,
    cen_v, cb_v, ybuf, idbuf, slotbuf, send, recv, labsend, labrecv, labrow, cent, cbk, cbp, acc,
    arsend, arrecv, finsend, finrecv,
    lsem, ysend, yrecv, isend, irecv, labs, labr, dsend, drecv, rss, rsr, ags, agr,
):
    n_list, n_sub, n_slab, n_lists, cols, groups, codes, width = dims
    owners = n_list * n_slab
    depth = groups * width
    slots = owners * CAP
    l, y, s = lax.axis_index("list"), lax.axis_index("sub"), lax.axis_index("slab")
    me = l * n_slab + s

    def plane(i):
        dl, ds = i // n_slab, lax.rem(i, n_slab)
        pl_, ps = lax.rem(l + dl, n_list), lax.rem(s + ds, n_slab)
        return (pl_, y, ps), pl_ * n_slab + ps

    offs = [0]
    for d in range(1, n_sub // 2 + 1):
        offs += [d] if 2 * d == n_sub else [d, n_sub - d]

    cen_copy = pltpu.make_async_copy(cen_ref, cen_v, lsem.at[0])
    cb_copy = pltpu.make_async_copy(cb_ref, cb_v, lsem.at[1])
    self_copy = pltpu.make_async_copy(
        vec_ref.at[pl.ds(pl.multiple_of(y * depth, depth), depth)], ybuf.at[0], lsem.at[2]
    )
    self_copy.start()
    cb_copy.start()
    cen_copy.start()

    bar = pltpu.get_barrier_semaphore()
    for d in range(1, n_sub):
        pl.semaphore_signal(bar, 1, device_id=(l, lax.rem(y + d, n_sub), s), device_id_type=MESH)

    def greet(i, _):
        pl.semaphore_signal(bar, 1, device_id=plane(i)[0], device_id_type=MESH)
        return 0

    lax.fori_loop(1, owners, greet, 0)

    earlier = (iota((cols, cols), 0) < iota((cols, cols), 1)).astype(BF16)

    def place(idrow):
        owner = idrow // n_lists
        hit = (iota((owners, cols), 0) == owner)
        before = dot(hit.astype(BF16), earlier)
        rank = jnp.sum(jnp.where(hit, before, 0.0), axis=0, keepdims=True).astype(I32)
        return hit, rank, owner * CAP + rank

    def pack(r):
        slot = slotbuf[r]
        put = (iota((slots, cols), 0) == slot).astype(BF16)
        a, b, c = split3(ybuf[r])
        send[r] = dot(put, a, 1, 1) + dot(put, b, 1, 1) + dot(put, c, 1, 1)

    def send_round(r):
        def go(i, _):
            dev, j = plane(i)
            pltpu.make_async_remote_copy(
                src_ref=send.at[r, pl.ds(pl.multiple_of(j * CAP, CAP), CAP)],
                dst_ref=recv.at[r, pl.ds(pl.multiple_of(me * CAP, CAP), CAP)],
                send_sem=dsend.at[r], recv_sem=drecv.at[r], device_id=dev, device_id_type=MESH,
            ).start()
            return 0

        lax.fori_loop(1, owners, go, 0)
        mine = pl.ds(pl.multiple_of(me * CAP, CAP), CAP)
        pltpu.make_async_copy(send.at[r, mine], recv.at[r, mine], lsem.at[3 + r]).start()

    idbuf[0] = ids_ref[...]
    slotbuf[0] = place(idbuf[0])[2]
    self_copy.wait()
    pack(0)

    pl.semaphore_wait(bar, owners - 1 + n_sub - 1)

    for r in range(1, n_sub):
        d = n_sub - offs[r]
        yy = lax.rem(y + d, n_sub)
        pltpu.make_async_remote_copy(
            src_ref=idbuf.at[0], dst_ref=idbuf.at[r],
            send_sem=isend, recv_sem=irecv, device_id=(l, yy, s), device_id_type=MESH,
        ).start()
    for r in range(1, n_sub):
        d = n_sub - offs[r]
        yy = lax.rem(y + d, n_sub)
        pltpu.make_async_remote_copy(
            src_ref=vec_ref.at[pl.ds(pl.multiple_of(yy * depth, depth), depth)], dst_ref=ybuf.at[r],
            send_sem=ysend, recv_sem=yrecv.at[r], device_id=(l, yy, s), device_id_type=MESH,
        ).start()
    send_round(0)

    cb_copy.wait()
    log2e = math.log2(math.e)
    for g in range(groups):
        cbt = jnp.swapaxes(cb_v[g], 0, 1)
        for h in range(codes // 128):
            for q in range(width // 4):
                cbp[(g * (codes // 128) + h) * (width // 4) + q, 0:4] = cbt[q * 4:q * 4 + 4, h * 128:h * 128 + 128]
        scaled = cbt * (2.0 / SOFTMAX_HEAT * log2e)
        norm = jnp.sum(cbt * cbt, axis=0, keepdims=True) * (-log2e / SOFTMAX_HEAT)
        c1, c2, c3 = (v.astype(F32) for v in split3(scaled))
        n1, n2, n3 = (v.astype(F32) for v in split3(norm))
        row = iota((16, codes), 0)
        tail = jnp.where(row == 0, n1, jnp.where(row == 1, n2, jnp.where(row == 2, n3, 0.0)))
        stack = jnp.concatenate([c1, c2, c3, c1, c2, c1, tail, jnp.zeros((256 - 6 * width - 16, codes), F32)], axis=0)
        cbk[g] = jnp.swapaxes(stack, 0, 1).astype(BF16)
    acc[...] = jnp.zeros_like(acc)

    whole = idbuf.at[pl.ds(1, n_sub - 1)]
    pltpu.make_async_copy(whole, whole, irecv).wait()
    labels = jnp.zeros((owners, 128), F32)
    for r in range(n_sub):
        idrow = idbuf[r]
        hit, rank, slot = place(idrow)
        if r:
            slotbuf[r] = slot
        number = idrow - (idrow // n_lists) * n_lists + 1
        high, low = (number // 64).astype(F32), (number % 64).astype(F32)
        q = iota((128, cols), 0) - (r * CAP)
        value = jnp.where(q == rank, high, jnp.where(q == rank + 32, low, 0.0)).astype(BF16)
        labels = labels + dot(hit.astype(BF16), value, 1, 1)
    labsend[...] = labels.reshape(owners, 1, 128)

    def send_labels(i, _):
        dev, j = plane(i)
        pltpu.make_async_remote_copy(
            src_ref=labsend.at[j], dst_ref=labrecv.at[me],
            send_sem=labs, recv_sem=labr, device_id=dev, device_id_type=MESH,
        ).start()
        return 0

    lax.fori_loop(1, owners, send_labels, 0)
    labrecv[me] = labsend[me]

    for r in range(1, n_sub):
        pltpu.make_async_copy(ybuf.at[r], ybuf.at[r], yrecv.at[r]).wait()
        pack(r)
        send_round(r)

    most = labrecv.at[pl.ds(0, owners - 1)]
    pltpu.make_async_copy(most, most, labr).wait()
    lab = labrecv[...].reshape(owners, 128).astype(BF16)
    from_j = iota((owners, slots), 1) // CAP == iota((owners, slots), 0)
    for r in range(n_sub):
        want = iota((128, slots), 1) % CAP + r * CAP
        q = iota((128, slots), 0)
        pick = jnp.where(q == want, 64.0, jnp.where(q == want + 32, 1.0, 0.0)).astype(BF16)
        labrow[r] = jnp.sum(jnp.where(from_j, dot(lab, pick), 0.0), axis=0, keepdims=True)
    cen_copy.wait()
    chunk = 512

    def gather(r, _):
        number = labrow[r].astype(I32) - 1
        total = jnp.zeros((depth, slots), F32)
        for k in range(n_lists // chunk):
            hot = (iota((chunk, slots), 0) == number - k * chunk).astype(BF16)
            total = total + dot(cen_v[:, k * chunk:(k + 1) * chunk], hot)
        cent[r] = total
        return 0

    lax.fori_loop(0, n_sub, gather, 0)

    def work(r, _):
        arrived = recv.at[r, pl.ds(0, slots - CAP)]
        pltpu.make_async_copy(arrived, arrived, drecv.at[r]).wait()
        mine = pl.ds(pl.multiple_of(me * CAP, CAP), CAP)
        pltpu.make_async_copy(send.at[r, mine], recv.at[r, mine], lsem.at[3 + r]).wait()
        present = (labrow[r] > 0.5).astype(F32)
        residual = jnp.swapaxes(recv[r], 0, 1) - cent[r]
        row = iota((16, slots), 0)
        ones = jnp.where(row < 3, 1.0, 0.0).astype(BF16)
        fill = jnp.zeros((256 - 6 * width - 16, slots), BF16)
        for g in range(groups):
            part = residual[g * width:(g + 1) * width]
            r1, r2, r3 = split3(part)
            stack = jnp.concatenate([r1, r1, r1, r2, r2, r3, ones, fill], axis=0)
            logits = dot(cbk[g], stack)
            e = jnp.exp2(logits - jnp.max(logits, axis=0, keepdims=True))
            inv = present / jnp.sum(e, axis=0, keepdims=True)
            w = jnp.concatenate([part * inv, jnp.where(row == 0, inv, 0.0)], axis=0)
            w = jnp.concatenate(split3(w), axis=0)
            e1 = e.astype(BF16)
            e2 = (e - e1.astype(F32)).astype(BF16)
            acc[g] += dot(w, e1, 1, 1) + dot(w, e2, 1, 1)
        return 0

    lax.fori_loop(0, n_sub, work, 0)

    part_rows = width + 16
    for g in range(groups):
        t = acc[g]
        t = t[0:part_rows] + t[part_rows:2 * part_rows] + t[2 * part_rows:3 * part_rows]
        for h in range(codes // 128):
            for q in range(width // 4):
                p = (g * (codes // 128) + h) * (width // 4) + q
                arsend[p, 0:4] = t[q * 4:q * 4 + 4, h * 128:h * 128 + 128]
                arsend[p, 4:5] = t[width:width + 1, h * 128:h * 128 + 128]

    def scatter(i, _):
        dev, j = plane(i)
        pltpu.make_async_remote_copy(
            src_ref=arsend.at[j, pl.ds(0, 5)], dst_ref=arrecv.at[me, pl.ds(0, 5)],
            send_sem=rss, recv_sem=rsr, device_id=dev, device_id_type=MESH,
        ).start()
        return 0

    lax.fori_loop(1, owners, scatter, 0)
    arrecv[me, 0:5] = arsend[me, 0:5]
    some = arrecv.at[pl.ds(0, owners - 1), pl.ds(0, 5)]
    pltpu.make_async_copy(some, some, rsr).wait()
    total = jnp.sum(arrecv[:, 0:5], axis=0)
    finsend[...] = (total[0:4] + PRIOR_MASS * cbp[me, 0:4]) / (total[4:5] + PRIOR_MASS)

    def hand(i, _):
        dev, j = plane(i)
        pltpu.make_async_remote_copy(
            src_ref=finsend, dst_ref=finrecv.at[me],
            send_sem=ags, recv_sem=agr, device_id=dev, device_id_type=MESH,
        ).start()
        return 0

    lax.fori_loop(1, owners, hand, 0)
    finrecv[me] = finsend[...]

    pltpu.make_async_copy(whole, whole, isend).wait()
    others = ybuf.at[pl.ds(1, n_sub - 1)]
    pltpu.make_async_copy(others, others, ysend).wait()
    pltpu.make_async_copy(most, most, labs).wait()
    for r in range(n_sub):
        gone = send.at[r, pl.ds(0, slots - CAP)]
        pltpu.make_async_copy(gone, gone, dsend.at[r]).wait()
    pltpu.make_async_copy(some, some, rss).wait()

    last = finrecv.at[pl.ds(0, owners - 1)]
    pltpu.make_async_copy(last, last, agr).wait()
    for g in range(groups):
        for h in range(codes // 128):
            for q in range(width // 4):
                p = (g * (codes // 128) + h) * (width // 4) + q
                out_ref[g, q * 4:q * 4 + 4, h * 128:h * 128 + 128] = finrecv[p]
    pltpu.make_async_copy(last, last, ags).wait()


def per_device(vectors, centroids, codebook, list_ids):
    n_list, n_sub, n_slab = (lax.axis_size(a) for a in ("list", "sub", "slab"))
    owners = n_list * n_slab
    n_lists, cols = centroids.shape[1], vectors.shape[1]
    groups, codes, width = codebook.shape
    depth = groups * width
    slots = owners * CAP
    dims = (n_list, n_sub, n_slab, n_lists, cols, groups, codes, width)
    dma = pltpu.SemaphoreType.DMA
    hbm = pl.BlockSpec(memory_space=pl.ANY)
    vmem = pl.BlockSpec(memory_space=pltpu.VMEM)
    out = pl.pallas_call(
        functools.partial(kernel, dims),
        out_shape=jax.ShapeDtypeStruct((groups, width, codes), F32),
        in_specs=[vmem, hbm, hbm, hbm],
        out_specs=vmem,
        scratch_shapes=[
            pltpu.VMEM((depth, n_lists), BF16),
            pltpu.VMEM((groups, codes, width), F32),
            pltpu.VMEM((n_sub, depth, cols), F32),
            pltpu.VMEM((n_sub, 1, cols), I32),
            pltpu.VMEM((n_sub, 1, cols), I32),
            pltpu.VMEM((n_sub, slots, depth), F32),
            pltpu.VMEM((n_sub, slots, depth), F32),
            pltpu.VMEM((owners, 1, 128), F32),
            pltpu.VMEM((owners, 1, 128), F32),
            pltpu.VMEM((n_sub, 1, slots), F32),
            pltpu.VMEM((n_sub, depth, slots), F32),
            pltpu.VMEM((groups, codes, 256), BF16),
            pltpu.VMEM((owners, 8, 128), F32),
            pltpu.VMEM((groups, 3 * (width + 16), codes), F32),
            pltpu.VMEM((owners, 8, 128), F32),
            pltpu.VMEM((owners, 8, 128), F32),
            pltpu.VMEM((4, 128), F32),
            pltpu.VMEM((owners, 4, 128), F32),
            dma((3 + n_sub,)), dma, dma((n_sub,)), dma, dma, dma, dma, dma((n_sub,)), dma((n_sub,)),
            dma, dma, dma, dma,
        ],
        compiler_params=pltpu.CompilerParams(
            collective_id=0, has_side_effects=True, vmem_limit_bytes=48 << 20
        ),
    )(list_ids.reshape(1, cols), vectors, centroids, codebook)
    return jnp.swapaxes(out, 1, 2)


def solution(mesh):
    return jax.shard_map(
        per_device,
        mesh=mesh,
        in_specs=(
            P(None, ("list", "sub", "slab")),
            P("sub", ("list", "slab")),
            P("sub", None, None),
            P(("list", "sub", "slab")),
        ),
        out_specs=P("sub", None, None),
        check_vma=False,
    )
```

time: 454 us -> 68.1 us (0.15)
  waiting for transfers between devices: 239 us -> 0 us
  blocking collectives: 123 us -> 0 us
  Pallas kernels: 0 us -> 64.8 us
  starting transfers between devices: 31.4 us -> 0 us
  matrix products: 20.1 us -> 0 us
  between operations: 13.6 us -> 0.04 us
  local copies, waits for them, and re-layouts: 15.3 us -> 3.04 us
  other arithmetic: 10.2 us -> 0 us
    psum x1 -> x0, waiting for transfers between devices: 182 us -> none  [per_device(): counts, weighted = lax.psum((counts, weighted), ('list', 'slab'))]
    psum x1 -> x0, blocking collectives: 123 us -> none  [per_device(): counts, weighted = lax.psum((counts, weighted), ('list', 'slab'))]
    pallas_call x0 -> x1, Pallas kernels: none -> 64.8 us  [per_device(): pl.pallas_call(functools.partial(kernel, dims), out_shape=jax.ShapeDtypeS...]
    all_to_all x4 -> x0, waiting for transfers between devices: 57.8 us -> none  [the longest x1 27.1 us: per_device(): lax.all_to_all(packed, ('list', 'slab'), split_axis=1, concat_axis=1, til...]
    all_to_all x4 -> x0, starting transfers between devices: 31.2 us -> none  [the longest x1 14.8 us: per_device(): lax.all_to_all(labels, ('list', 'slab'), split_axis=1, concat_axis=1, til...]
    dot_general x5 -> x0, matrix products: 20.1 us -> none  [the longest x2 13 us: block_step(): jnp.einsum('skn,sdn->skd', assign, column_piece, precision=lax.Precision....]
    gather x1 -> x0, local copies, waits for them, and re-layouts: 6.18 us -> none  [per_device(): nearest = jnp.take(centroids, list_index, axis=1).astype(jnp.float32)]
    sub x3 -> x0, other arithmetic: 5.99 us -> none  [the longest x2 5.99 us: block_step(): assignment_scores - jnp.max(assignment_scores, axis=1, keepdims=True)]
  transfers between devices with their start and end apart: 5 -> 0, of which waited for: 5 -> 0; matrix products, arithmetic and copies ran while one was open for 2% -> 0% of each run, Pallas kernels for 0% -> 0%
where the time goes in v1:
time: 68.1 us; the launch traced here: 67.9 us
  Pallas kernels  64.8 us (95%)
  local copies, waits for them, and re-layouts  3.04 us (4%)
    pallas_call x1, Pallas kernels, per_device(): pl.pallas_call(functools.partial(kernel, dims), out_shape=jax.ShapeDtypeS...  64.8 us
    unnamed x8, local copies, waits for them, and re-layouts  3.04 us

profile of v1, /device:TPU:1, one launch (start us, length us, event | category | flops | bytes accessed | tf_op | source)
XLA Modules:
  0.0 67.9 jit_solution(17849818228151396867)
XLA Ops:
  0.0 0.0 copy-start.1
  0.0 0.0 copy-start.2
  0.0 1.2 %copy.5.cb_ref = f32[4,256,32]{2,1,0:T(8,128)S(1)} copy(f32[4,256,32]{1,2,0:T(8,128)} %param.6) | data formatting | bytes 262144 | tf_op args[2]
  1.2 0.0 copy-done.1
  1.2 0.0 copy-done.2
  1.2 0.0 copy-start
  1.2 1.2 %copy-done = bf16[128,4096]{1,0:T(8,128)(2,1)S(1)} copy-done((bf16[128,4096]{1,0:T(8,128)(2,1)S(1)}, bf16[128,4096]{1,0:T(8,128)(2,1)}, u32[]{:S(2)}) %copy-start) | copy-done | bytes 1048600
  2.4 64.8 %shard_map.46 = f32[4,32,256]{2,1,0:T(8,128)S(1)} custom-call(s32[1,128]{1,0:T(1,128)S(1)} %bitcast.3, f32[1024,128]{1,0:T(8,128)S(1)} %copy-done.1, bf16[128,4096]{1,0:T(8,128)(2,1)S(1)} %copy-done, f32[4,256,32]{2,1,0:T(8,128)S(1)} %copy.5.cb_ref), custom_call_target="tpu_custom_call" | custom-call | tf_op jit(solution)/shard_map/pallas_call | solution.py:292
  67.3 0.7 copy.7
Async XLA Ops:
  0.0 1.2 %copy-start.1 = (f32[1024,128]{1,0:T(8,128)S(1)}, f32[1024,128]{1,0:T(8,128)}, u32[]{:S(2)}) copy-start(f32[1024,128]{1,0:T(8,128)} %vec_ref.1) | copy-start | bytes 1572868
  0.0 1.2 %copy-start.2 = (s32[128]{0:T(128)S(1)}, s32[128]{0:T(128)}, u32[]{:S(2)}) copy-start(s32[128]{0:T(128)} %param.7) | copy-start | bytes 1540
  1.2 1.2 %copy-start = (bf16[128,4096]{1,0:T(8,128)(2,1)S(1)}, bf16[128,4096]{1,0:T(8,128)(2,1)}, u32[]{:S(2)}) copy-start(bf16[128,4096]{1,0:T(8,128)(2,1)} %cen_ref.1) | copy-start | bytes 3145732

commit v2 on v1

v2 whole, which is shorter than its diff:
```python
import functools
import math

import jax
import jax.numpy as jnp
from jax import lax
from jax.experimental import pallas as pl
from jax.experimental.pallas import tpu as pltpu
from jax.sharding import PartitionSpec as P

SOFTMAX_HEAT = 8.0
PRIOR_MASS = 1.0
MESH = pl.DeviceIdType.MESH
F32, BF16, I32 = jnp.float32, jnp.bfloat16, jnp.int32
GROUPS = ((0,), (1,), (2, 3), (4, 5), (6, 7))
CAP = 4


def split3(x):
    a = x.astype(BF16)
    rest = x - a.astype(F32)
    b = rest.astype(BF16)
    c = (rest - b.astype(F32)).astype(BF16)
    return a, b, c


def dot(a, b, ca=1, cb=0):
    return lax.dot_general(a, b, (((ca,), (cb,)), ((), ())), preferred_element_type=F32)


def iota(shape, dim):
    return lax.broadcasted_iota(I32, shape, dim)


def kernel(
    dims,
    ids_ref, vec_ref, cen_ref, cb_ref,
    out_ref,
    cen_v, cb_v, ybuf, idbuf, ownbuf, rankbuf, send, recv, labsend, labrecv, labrow, cent, cbk, cbp, acc,
    arsend, arrecv, zsend, zrecv, finsend, finrecv,
    lsem, ysend, yrecv, isend, irecv, labs, labr, dsend, drecv, ars, arr,
):
    n_list, n_sub, n_slab, n_lists, cols, groups, codes, width = dims
    owners = n_list * n_slab
    depth = groups * width
    slots = owners * CAP
    l, y, s = lax.axis_index("list"), lax.axis_index("sub"), lax.axis_index("slab")
    me = l * n_slab + s

    cores, half = 2, n_list // 2
    far_first = sorted(range(n_slab), key=lambda d: -min(d, n_slab - d))
    slabs = [lax.rem(s + ds, n_slab) for ds in far_first]

    def wrap(v, n):
        return jnp.where(v >= n, v - n, v)

    def each_owner(do):
        def one_list(there, which):
            for w in which:
                do((there, y, slabs[w]), there * n_slab + slabs[w])

        one_list(wrap(l + half, n_list), range(n_slab))

        def two_lists(t, _):
            one_list(wrap(l + (half - t), n_list), range(n_slab))
            one_list(wrap(l + (half + t), n_list), range(n_slab))
            return 0

        lax.fori_loop(1, half, two_lists, 0)
        one_list(l, [w for w in range(n_slab) if far_first[w]])

    offs = [0]
    for d in range(1, n_sub // 2 + 1):
        offs += [d] if 2 * d == n_sub else [d, n_sub - d]

    parts = GROUPS if n_sub == 8 else tuple((r,) for r in range(n_sub))

    cen_copy = pltpu.make_async_copy(cen_ref, cen_v, lsem.at[0])
    cb_copy = pltpu.make_async_copy(cb_ref, cb_v, lsem.at[1])
    self_copy = pltpu.make_async_copy(
        vec_ref.at[pl.ds(pl.multiple_of(y * depth, depth), depth)], ybuf.at[0], lsem.at[2]
    )
    ids_copy = pltpu.make_async_copy(ids_ref, idbuf.at[0], lsem.at[3 + n_sub])
    ids_copy.start()
    self_copy.start()
    cb_copy.start()
    cen_copy.start()

    bar = pltpu.get_barrier_semaphore()
    each_owner(lambda dev, j: pl.semaphore_signal(bar, 1, device_id=dev, device_id_type=MESH))
    for d in range(1, n_sub):
        pl.semaphore_signal(bar, 1, device_id=(l, lax.rem(y + d, n_sub), s), device_id_type=MESH)


    earlier = (iota((cols, cols), 0) < iota((cols, cols), 1)).astype(BF16)

    def place(r):
        idrow = idbuf[r]
        owner = idrow // n_lists
        hit = (iota((owners, cols), 0) == owner)
        before = dot(hit.astype(BF16), earlier)
        rank = jnp.sum(jnp.where(hit, before, 0.0), axis=0, keepdims=True).astype(I32)
        number = idrow - owner * n_lists + 1
        return hit, rank, owner, number

    def rows_of(p):
        return parts[p][0] * slots, len(parts[p]) * slots

    def pack(p):
        base, count = rows_of(p)
        each = len(parts[p]) * CAP
        row = iota((count, cols), 0)
        total = None
        for i, r in enumerate(parts[p]):
            put = (row == ownbuf[r] * each + rankbuf[r] + i * CAP).astype(BF16)
            for v in split3(ybuf[r]):
                term = dot(put, v, 1, 1)
                total = term if total is None else total + term
        send[base:base + count] = total

    def send_part(p):
        base, count = rows_of(p)
        each = len(parts[p]) * CAP

        def go(dev, j):
            pltpu.make_async_remote_copy(
                src_ref=send.at[pl.ds(pl.multiple_of(base + j * each, CAP), each)],
                dst_ref=recv.at[pl.ds(pl.multiple_of(base + me * each, CAP), each)],
                send_sem=dsend.at[p], recv_sem=drecv.at[p], device_id=dev, device_id_type=MESH,
            ).start()

        each_owner(go)
        own_part(p).start()

    def own_part(p):
        base, _ = rows_of(p)
        each = len(parts[p]) * CAP
        mine = pl.ds(pl.multiple_of(base + me * each, CAP), each)
        return pltpu.make_async_copy(send.at[mine], recv.at[mine], lsem.at[3 + p])

    ids_copy.wait()
    _, rankbuf[0], ownbuf[0], _ = place(0)
    self_copy.wait()
    pack(0)

    pl.semaphore_wait(bar, owners - 1 + n_sub - 1)

    for r in range(1, n_sub):
        d = n_sub - offs[r]
        yy = lax.rem(y + d, n_sub)
        pltpu.make_async_remote_copy(
            src_ref=idbuf.at[0], dst_ref=idbuf.at[r],
            send_sem=isend, recv_sem=irecv, device_id=(l, yy, s), device_id_type=MESH,
        ).start()
    for r in range(1, n_sub):
        d = n_sub - offs[r]
        yy = lax.rem(y + d, n_sub)
        pltpu.make_async_remote_copy(
            src_ref=vec_ref.at[pl.ds(pl.multiple_of(yy * depth, depth), depth)], dst_ref=ybuf.at[r],
            send_sem=ysend, recv_sem=yrecv.at[r], device_id=(l, yy, s), device_id_type=MESH,
        ).start()
    send_part(0)

    whole = idbuf.at[pl.ds(1, n_sub - 1)]
    pltpu.make_async_copy(whole, whole, irecv).wait()
    labels = jnp.zeros((owners, 128), F32)
    for r in range(n_sub):
        hit, rank, owner, number = place(r)
        if r:
            rankbuf[r], ownbuf[r] = rank, owner
        high, low = (number // 64).astype(F32), (number % 64).astype(F32)
        q = iota((128, cols), 0) - (r * CAP)
        value = jnp.where(q == rank, high, jnp.where(q == rank + 32, low, 0.0)).astype(BF16)
        labels = labels + dot(hit.astype(BF16), value, 1, 1)
    labsend[...] = labels.reshape(owners, 1, 128)
    labrecv[me] = labsend[me]

    def send_labels(dev, j):
        pltpu.make_async_remote_copy(
            src_ref=labsend.at[j], dst_ref=labrecv.at[me],
            send_sem=labs, recv_sem=labr, device_id=dev, device_id_type=MESH,
        ).start()

    for p in range(1, len(parts)):
        for r in parts[p]:
            pltpu.make_async_copy(ybuf.at[r], ybuf.at[r], yrecv.at[r]).wait()
        pack(p)
        send_part(p)
        if p == 1:
            each_owner(send_labels)

    cb_copy.wait()
    log2e = math.log2(math.e)
    for g in range(groups):
        cbt = cb_v[g]
        for h in range(codes // 128):
            cbp[g * (codes // 128) + h] = cbt[:, h * 128:h * 128 + 128]
        scaled = cbt * (2.0 / SOFTMAX_HEAT * log2e)
        norm = jnp.sum(cbt * cbt, axis=0, keepdims=True) * (-log2e / SOFTMAX_HEAT)
        c1, c2, c3 = (v.astype(F32) for v in split3(scaled))
        n1, n2, n3 = (v.astype(F32) for v in split3(norm))
        row = iota((16, codes), 0)
        tail = jnp.where(row == 0, n1, jnp.where(row == 1, n2, jnp.where(row == 2, n3, 0.0)))
        stack = jnp.concatenate([c1, c2, c3, c1, c2, c1, tail, jnp.zeros((256 - 6 * width - 16, codes), F32)], axis=0)
        cbk[g] = jnp.swapaxes(stack, 0, 1).astype(BF16)
    acc[...] = jnp.zeros_like(acc)

    most = labrecv.at[pl.ds(0, owners - 1)]
    pltpu.make_async_copy(most, most, labr).wait()
    lab = labrecv[...].reshape(owners, 128).astype(BF16)
    for p, members in enumerate(parts):
        each = len(members) * CAP
        for b in range(len(members)):
            lane = iota((128, slots), 1) + b * slots
            want = lane % each + members[0] * CAP
            q = iota((128, slots), 0)
            pick = jnp.where(q == want, 64.0, jnp.where(q == want + 32, 1.0, 0.0)).astype(BF16)
            from_j = (iota((owners, slots), 1) + b * slots) // each == iota((owners, slots), 0)
            labrow[members[b]] = jnp.sum(jnp.where(from_j, dot(lab, pick), 0.0), axis=0, keepdims=True)
    cen_copy.wait()
    chunk = 512

    def gather(r, _):
        number = labrow[r].astype(I32) - 1
        total = jnp.zeros((depth, slots), F32)
        for k in range(n_lists // chunk):
            hot = (iota((chunk, slots), 0) == number - k * chunk).astype(BF16)
            total = total + dot(cen_v[:, k * chunk:(k + 1) * chunk], hot)
        cent[r] = total
        return 0

    lax.fori_loop(0, n_sub, gather, 0)

    def work(r, _):
        present = (labrow[r] > 0.5).astype(F32)
        residual = jnp.swapaxes(recv[pl.ds(pl.multiple_of(r * slots, slots), slots)], 0, 1) - cent[r]
        row = iota((16, slots), 0)
        ones = jnp.where(row < 3, 1.0, 0.0).astype(BF16)
        fill = jnp.zeros((256 - 6 * width - 16, slots), BF16)
        for g in range(groups):
            part = residual[g * width:(g + 1) * width]
            r1, r2, r3 = split3(part)
            stack = jnp.concatenate([r1, r1, r1, r2, r2, r3, ones, fill], axis=0)
            logits = dot(cbk[g], stack)
            e = jnp.exp2(logits - jnp.max(logits, axis=0, keepdims=True))
            inv = present / jnp.sum(e, axis=0, keepdims=True)
            w = jnp.concatenate([part * inv, jnp.where(row == 0, inv, 0.0)], axis=0)
            w = jnp.concatenate(split3(w), axis=0)
            e1 = e.astype(BF16)
            e2 = (e - e1.astype(F32)).astype(BF16)
            acc[g] += dot(w, e1, 1, 1) + dot(w, e2, 1, 1)
        return 0

    for p, members in enumerate(parts):
        base, count = rows_of(p)
        arrived = recv.at[pl.ds(base, count - len(members) * CAP)]
        pltpu.make_async_copy(arrived, arrived, drecv.at[p]).wait()
        own_part(p).wait()
        if len(members) == 1:
            work(members[0], 0)
        else:
            lax.fori_loop(members[0], members[-1] + 1, work, 0)

    z, core = l // cores, lax.rem(l, cores)
    n_z, n_k = n_list // cores, n_slab * cores
    k = s * cores + core
    part_rows = width + 16
    for g in range(groups):
        t = acc[g]
        t = t[0:width + 8] + t[part_rows:part_rows + width + 8] + t[2 * part_rows:2 * part_rows + width + 8]
        for h in range(codes // 128):
            arsend[g * (codes // 128) + h] = t[:, h * 128:h * 128 + 128]

    def along_k(i):
        to_s = lax.rem(s + i // cores, n_slab)
        to_c = lax.rem(core + i, cores)
        return (z * cores + to_c, y, to_s), to_s * cores + to_c

    order_k = sorted(range(1, n_k), key=lambda i: -min(i // cores, n_slab - i // cores))
    order_z = sorted(range(1, n_z), key=lambda i: -min(i, n_z - i))
    rows = width + 1
    for i in order_k:
        dev, j = along_k(i)
        pltpu.make_async_remote_copy(
            src_ref=arsend.at[j, pl.ds(0, rows)], dst_ref=arrecv.at[k, pl.ds(0, rows)],
            send_sem=ars.at[0], recv_sem=arr.at[0], device_id=dev, device_id_type=MESH,
        ).start()
    arrecv[k] = arsend[k]
    got_k = arrecv.at[pl.ds(0, n_k - 1), pl.ds(0, rows)]
    pltpu.make_async_copy(got_k, got_k, arr.at[0]).wait()
    zsend[...] = jnp.sum(arrecv[...], axis=0)
    for i in order_z:
        pltpu.make_async_remote_copy(
            src_ref=zsend.at[pl.ds(0, rows)], dst_ref=zrecv.at[z, pl.ds(0, rows)],
            send_sem=ars.at[1], recv_sem=arr.at[1],
            device_id=(lax.rem(z + i, n_z) * cores + core, y, s), device_id_type=MESH,
        ).start()
    zrecv[z] = zsend[...]
    got_z = zrecv.at[pl.ds(0, n_z - 1), pl.ds(0, rows)]
    pltpu.make_async_copy(got_z, got_z, arr.at[1]).wait()
    total = jnp.sum(zrecv[...], axis=0)
    finsend[...] = (total[0:width] + PRIOR_MASS * cbp[k]) / (total[width:width + 1] + PRIOR_MASS)
    for i in order_k:
        dev, j = along_k(i)
        pltpu.make_async_remote_copy(
            src_ref=finsend, dst_ref=finrecv.at[k],
            send_sem=ars.at[2], recv_sem=arr.at[2], device_id=dev, device_id_type=MESH,
        ).start()
    finrecv[k] = finsend[...]

    pltpu.make_async_copy(whole, whole, isend).wait()
    others = ybuf.at[pl.ds(1, n_sub - 1)]
    pltpu.make_async_copy(others, others, ysend).wait()
    pltpu.make_async_copy(most, most, labs).wait()
    for p, members in enumerate(parts):
        base, count = rows_of(p)
        gone = send.at[pl.ds(base, count - len(members) * CAP)]
        pltpu.make_async_copy(gone, gone, dsend.at[p]).wait()
    pltpu.make_async_copy(got_k, got_k, ars.at[0]).wait()
    pltpu.make_async_copy(got_z, got_z, ars.at[1]).wait()

    last = finrecv.at[pl.ds(0, n_k - 1)]
    pltpu.make_async_copy(last, last, arr.at[2]).wait()
    for g in range(groups):
        for h in range(codes // 128):
            out_ref[g, :, h * 128:h * 128 + 128] = finrecv[g * (codes // 128) + h]
    pltpu.make_async_copy(last, last, ars.at[2]).wait()


def per_device(vectors, centroids, codebook, list_ids):
    n_list, n_sub, n_slab = (lax.axis_size(a) for a in ("list", "sub", "slab"))
    owners = n_list * n_slab
    n_lists, cols = centroids.shape[1], vectors.shape[1]
    groups, codes, width = codebook.shape
    depth = groups * width
    slots = owners * CAP
    n_z, n_k = n_list // 2, n_slab * 2
    dims = (n_list, n_sub, n_slab, n_lists, cols, groups, codes, width)
    dma = pltpu.SemaphoreType.DMA
    hbm = pl.BlockSpec(memory_space=pl.ANY)
    vmem = pl.BlockSpec(memory_space=pltpu.VMEM)
    out = pl.pallas_call(
        functools.partial(kernel, dims),
        out_shape=jax.ShapeDtypeStruct((groups, width, codes), F32),
        in_specs=[hbm, hbm, hbm, hbm],
        out_specs=vmem,
        scratch_shapes=[
            pltpu.VMEM((depth, n_lists), BF16),
            pltpu.VMEM((groups, width, codes), F32),
            pltpu.VMEM((n_sub, depth, cols), F32),
            pltpu.VMEM((n_sub, 1, cols), I32),
            pltpu.VMEM((n_sub, 1, cols), I32),
            pltpu.VMEM((n_sub, 1, cols), I32),
            pltpu.VMEM((n_sub * slots, depth), F32),
            pltpu.VMEM((n_sub * slots, depth), F32),
            pltpu.VMEM((owners, 1, 128), F32),
            pltpu.VMEM((owners, 1, 128), F32),
            pltpu.VMEM((n_sub, 1, slots), F32),
            pltpu.VMEM((n_sub, depth, slots), F32),
            pltpu.VMEM((groups, codes, 256), BF16),
            pltpu.VMEM((n_k, width, 128), F32),
            pltpu.VMEM((groups, 3 * (width + 16), codes), F32),
            pltpu.VMEM((n_k, width + 8, 128), F32),
            pltpu.VMEM((n_k, width + 8, 128), F32),
            pltpu.VMEM((width + 8, 128), F32),
            pltpu.VMEM((n_z, width + 8, 128), F32),
            pltpu.VMEM((width, 128), F32),
            pltpu.VMEM((n_k, width, 128), F32),
            dma((4 + n_sub,)), dma, dma((n_sub,)), dma, dma, dma, dma, dma((n_sub,)), dma((n_sub,)),
            dma((3,)), dma((3,)),
        ],
        compiler_params=pltpu.CompilerParams(
            collective_id=0, has_side_effects=True, vmem_limit_bytes=60 << 20
        ),
    )(list_ids.reshape(1, cols), vectors, centroids, jnp.swapaxes(codebook, 1, 2))
    return jnp.swapaxes(out, 1, 2)


def solution(mesh):
    return jax.shard_map(
        per_device,
        mesh=mesh,
        in_specs=(
            P(None, ("list", "sub", "slab")),
            P("sub", ("list", "slab")),
            P("sub", None, None),
            P(("list", "sub", "slab")),
        ),
        out_specs=P("sub", None, None),
        check_vma=False,
    )
```

time: 68.1 us -> 64 us (0.940)
  Pallas kernels: 64.8 us -> 62.3 us
  local copies, waits for them, and re-layouts: 3.04 us -> 1.57 us
    pallas_call x1, Pallas kernels: 64.8 us -> 62.3 us  [per_device(): pl.pallas_call(functools.partial(kernel, dims), out_shape=jax.ShapeDtypeS...]
    unnamed x8 -> x1, local copies, waits for them, and re-layouts: 3.04 us -> 1.57 us
where the time goes in v2:
time: 64 us; the launch traced here: 63.9 us
  Pallas kernels  62.3 us (97%)
  local copies, waits for them, and re-layouts  1.57 us (2%)
    pallas_call x1, Pallas kernels, per_device(): pl.pallas_call(functools.partial(kernel, dims), out_shape=jax.ShapeDtypeS...  62.3 us
    unnamed x1, local copies, waits for them, and re-layouts  1.57 us

profile of v2, /device:TPU:1, one launch (start us, length us, event | category | flops | bytes accessed | tf_op | source)
XLA Modules:
  0.0 63.9 jit_solution(8339538862435394693)
XLA Ops:
  0.0 62.3 %shard_map.46 = f32[4,32,256]{2,1,0:T(8,128)} custom-call(s32[1,128]{1,0:T(1,128)} %bitcast.5, f32[1024,128]{1,0:T(8,128)} %vec_ref.1, bf16[128,4096]{1,0:T(8,128)(2,1)} %cen_ref.1, f32[4,32,256]{2,1,0:T(8,128)} %bitcast.4), custom_call_target="tpu_custom_call" | custom-call | tf_op jit(solution)/shard_map/pallas_call | solution.py:342
  62.3 1.6 %copy.6 = f32[4,256,32]{1,2,0:T(8,128)} copy(f32[4,256,32]{1,2,0:T(8,128)} %bitcast.3) | data formatting | bytes 262144

commit v3 on v2

--- a/solution.py
+++ b/solution.py
@@ -12,7 +12,7 @@
 PRIOR_MASS = 1.0
 MESH = pl.DeviceIdType.MESH
 F32, BF16, I32 = jnp.float32, jnp.bfloat16, jnp.int32
-GROUPS = ((0,), (1,), (2, 3), (4, 5), (6, 7))
+GROUPS = ((0,), (1,), (2,), (3, 4), (5, 6), (7,))
 CAP = 4
 
 
@@ -231,31 +231,42 @@
 
     lax.fori_loop(0, n_sub, gather, 0)
 
-    def work(r, _):
+    row = iota((16, slots), 0)
+
+    def prepare(r):
         present = (labrow[r] > 0.5).astype(F32)
-        residual = jnp.swapaxes(recv[pl.ds(pl.multiple_of(r * slots, slots), slots)], 0, 1) - cent[r]
-        row = iota((16, slots), 0)
+        arrived = recv[pl.ds(pl.multiple_of(r * slots, slots), slots)]
+        return present, jnp.swapaxes(arrived, 0, 1) - cent[r]
+
+    def sums(g, present, residual):
+        part = residual[g * width:(g + 1) * width]
+        r1, r2, r3 = split3(part)
         ones = jnp.where(row < 3, 1.0, 0.0).astype(BF16)
         fill = jnp.zeros((256 - 6 * width - 16, slots), BF16)
+        stack = jnp.concatenate([r1, r1, r1, r2, r2, r3, ones, fill], axis=0)
+        logits = dot(cbk[g], stack)
+        e = jnp.exp2(logits - jnp.max(logits, axis=0, keepdims=True))
+        inv = present / jnp.sum(e, axis=0, keepdims=True)
+        w = jnp.concatenate([part * inv, jnp.where(row == 0, inv, 0.0)], axis=0)
+        w = jnp.concatenate(split3(w), axis=0)
+        e1 = e.astype(BF16)
+        e2 = (e - e1.astype(F32)).astype(BF16)
+        return dot(w, e1, 1, 1) + dot(w, e2, 1, 1)
+
+    def work(r, _):
+        present, residual = prepare(r)
         for g in range(groups):
-            part = residual[g * width:(g + 1) * width]
-            r1, r2, r3 = split3(part)
-            stack = jnp.concatenate([r1, r1, r1, r2, r2, r3, ones, fill], axis=0)
-            logits = dot(cbk[g], stack)
-            e = jnp.exp2(logits - jnp.max(logits, axis=0, keepdims=True))
-            inv = present / jnp.sum(e, axis=0, keepdims=True)
-            w = jnp.concatenate([part * inv, jnp.where(row == 0, inv, 0.0)], axis=0)
-            w = jnp.concatenate(split3(w), axis=0)
-            e1 = e.astype(BF16)
-            e2 = (e - e1.astype(F32)).astype(BF16)
-            acc[g] += dot(w, e1, 1, 1) + dot(w, e2, 1, 1)
+            acc[g] += sums(g, present, residual)
         return 0
 
-    for p, members in enumerate(parts):
+    def arrival(p):
         base, count = rows_of(p)
-        arrived = recv.at[pl.ds(base, count - len(members) * CAP)]
+        arrived = recv.at[pl.ds(base, count - len(parts[p]) * CAP)]
         pltpu.make_async_copy(arrived, arrived, drecv.at[p]).wait()
         own_part(p).wait()
+
+    for p, members in enumerate(parts[:-1]):
+        arrival(p)
         if len(members) == 1:
             work(members[0], 0)
         else:
@@ -264,12 +275,7 @@
     z, core = l // cores, lax.rem(l, cores)
     n_z, n_k = n_list // cores, n_slab * cores
     k = s * cores + core
-    part_rows = width + 16
-    for g in range(groups):
-        t = acc[g]
-        t = t[0:width + 8] + t[part_rows:part_rows + width + 8] + t[2 * part_rows:2 * part_rows + width + 8]
-        for h in range(codes // 128):
-            arsend[g * (codes // 128) + h] = t[:, h * 128:h * 128 + 128]
+    rows, blocks = width + 1, codes // 128
 
     def along_k(i):
         to_s = lax.rem(s + i // cores, n_slab)
@@ -278,13 +284,26 @@
 
     order_k = sorted(range(1, n_k), key=lambda i: -min(i // cores, n_slab - i // cores))
     order_z = sorted(range(1, n_z), key=lambda i: -min(i, n_z - i))
-    rows = width + 1
-    for i in order_k:
-        dev, j = along_k(i)
+
+    def give(j):
         pltpu.make_async_remote_copy(
             src_ref=arsend.at[j, pl.ds(0, rows)], dst_ref=arrecv.at[k, pl.ds(0, rows)],
-            send_sem=ars.at[0], recv_sem=arr.at[0], device_id=dev, device_id_type=MESH,
-        ).start()
+            send_sem=ars.at[0], recv_sem=arr.at[0],
+            device_id=(z * cores + j % cores, y, j // cores), device_id_type=MESH,
+        ).start()
+
+    for p in range(len(parts) - 1, len(parts)):
+        arrival(p)
+        for r in parts[p][:-1]:
+            work(r, 0)
+        present, residual = prepare(parts[p][-1])
+        for g in range(groups):
+            t = acc[g] + sums(g, present, residual)
+            t = sum(t[i * (width + 16):i * (width + 16) + width + 8] for i in range(3))
+            for h in range(blocks):
+                j = g * blocks + h
+                arsend[j] = t[:, h * 128:h * 128 + 128]
+                pl.when(k != j)(functools.partial(give, j))
     arrecv[k] = arsend[k]
     got_k = arrecv.at[pl.ds(0, n_k - 1), pl.ds(0, rows)]
     pltpu.make_async_copy(got_k, got_k, arr.at[0]).wait()
@@ -341,7 +360,7 @@
     vmem = pl.BlockSpec(memory_space=pltpu.VMEM)
     out = pl.pallas_call(
         functools.partial(kernel, dims),
-        out_shape=jax.ShapeDtypeStruct((groups, width, codes), F32),
+        out_shape=pltpu.VMEM((groups, width, codes), F32),
         in_specs=[hbm, hbm, hbm, hbm],
         out_specs=vmem,
         scratch_shapes=[

time: 64 us -> 62.5 us (0.977)
  local copies, waits for them, and re-layouts: 1.57 us -> 0.66 us
    unnamed x1, local copies, waits for them, and re-layouts: 1.57 us -> 0.66 us
where the time goes in v3:
time: 62.5 us; the launch traced here: 62.4 us
  Pallas kernels  61.7 us (99%)
  local copies, waits for them, and re-layouts  0.66 us (1%)
    pallas_call x1, Pallas kernels, per_device(): pl.pallas_call(functools.partial(kernel, dims), out_shape=pltpu.VMEM((gro...  61.7 us

profile of v3, /device:TPU:1, one launch (start us, length us, event | category | flops | bytes accessed | tf_op | source)
XLA Modules:
  0.0 62.4 jit_solution(16383427243720767572)
XLA Ops:
  0.0 61.7 %shard_map.46 = f32[4,32,256]{2,1,0:T(8,128)S(1)} custom-call(s32[1,128]{1,0:T(1,128)} %bitcast.5, f32[1024,128]{1,0:T(8,128)} %vec_ref.1, bf16[128,4096]{1,0:T(8,128)(2,1)} %cen_ref.1, f32[4,32,256]{2,1,0:T(8,128)} %bitcast.4), custom_call_target="tpu_custom_call" | custom-call | tf_op jit(solution)/shard_map/pallas_call | solution.py:361
  61.7 0.7 %copy.6 = f32[4,256,32]{1,2,0:T(8,128)} copy(f32[4,256,32]{1,2,0:T(8,128)S(1)} %bitcast.3) | data formatting | bytes 262144

commit v4 on v3

--- a/solution.py
+++ b/solution.py
@@ -152,6 +152,7 @@
             src_ref=idbuf.at[0], dst_ref=idbuf.at[r],
             send_sem=isend, recv_sem=irecv, device_id=(l, yy, s), device_id_type=MESH,
         ).start()
+    send_part(0)
     for r in range(1, n_sub):
         d = n_sub - offs[r]
         yy = lax.rem(y + d, n_sub)
@@ -159,7 +160,6 @@
             src_ref=vec_ref.at[pl.ds(pl.multiple_of(yy * depth, depth), depth)], dst_ref=ybuf.at[r],
             send_sem=ysend, recv_sem=yrecv.at[r], device_id=(l, yy, s), device_id_type=MESH,
         ).start()
-    send_part(0)
 
     whole = idbuf.at[pl.ds(1, n_sub - 1)]
     pltpu.make_async_copy(whole, whole, irecv).wait()
@@ -181,14 +181,87 @@
             send_sem=labs, recv_sem=labr, device_id=dev, device_id_type=MESH,
         ).start()
 
-    for p in range(1, len(parts)):
+    def move_on(p):
         for r in parts[p]:
             pltpu.make_async_copy(ybuf.at[r], ybuf.at[r], yrecv.at[r]).wait()
         pack(p)
         send_part(p)
-        if p == 1:
+        if p == 2:
             each_owner(send_labels)
 
+    row = iota((16, slots), 0)
+
+    def prepare(r):
+        present = (labrow[r] > 0.5).astype(F32)
+        arrived = recv[pl.ds(pl.multiple_of(r * slots, slots), slots)]
+        return present, jnp.swapaxes(arrived, 0, 1) - cent[r]
+
+    def sums(g, present, residual):
+        part = residual[g * width:(g + 1) * width]
+        r1, r2, r3 = split3(part)
+        ones = jnp.where(row < 3, 1.0, 0.0).astype(BF16)
+        fill = jnp.zeros((256 - 6 * width - 16, slots), BF16)
+        stack = jnp.concatenate([r1, r1, r1, r2, r2, r3, ones, fill], axis=0)
+        logits = dot(cbk[g], stack)
+        e = jnp.exp2(logits - jnp.max(logits, axis=0, keepdims=True))
+        inv = present / jnp.sum(e, axis=0, keepdims=True)
+        w = jnp.concatenate([part * inv, jnp.where(row == 0, inv, 0.0)], axis=0)
+        w = jnp.concatenate(split3(w), axis=0)
+        e1 = e.astype(BF16)
+        e2 = (e - e1.astype(F32)).astype(BF16)
+        return dot(w, e1, 1, 1) + dot(w, e2, 1, 1)
+
+    def work(r, _):
+        present, residual = prepare(r)
+        for g in range(groups):
+            acc[g] += sums(g, present, residual)
+        return 0
+
+    def arrival(p):
+        base, count = rows_of(p)
+        arrived = recv.at[pl.ds(base, count - len(parts[p]) * CAP)]
+        pltpu.make_async_copy(arrived, arrived, drecv.at[p]).wait()
+        own_part(p).wait()
+
+    def work_part(p):
+        members = parts[p]
+        arrival(p)
+        if len(members) == 1:
+            work(members[0], 0)
+        else:
+            lax.fori_loop(members[0], members[-1] + 1, work, 0)
+
+    move_on(1)
+    move_on(2)
+    move_on(3)
+    move_on(4)
+    most = labrecv.at[pl.ds(0, owners - 1)]
+    pltpu.make_async_copy(most, most, labr).wait()
+    lab = labrecv[...].reshape(owners, 128).astype(BF16)
+    for p, members in enumerate(parts):
+        each = len(members) * CAP
+        for b in range(len(members)):
+            lane = iota((128, slots), 1) + b * slots
+            want = lane % each + members[0] * CAP
+            q = iota((128, slots), 0)
+            pick = jnp.where(q == want, 64.0, jnp.where(q == want + 32, 1.0, 0.0)).astype(BF16)
+            from_j = (iota((owners, slots), 1) + b * slots) // each == iota((owners, slots), 0)
+            labrow[members[b]] = jnp.sum(jnp.where(from_j, dot(lab, pick), 0.0), axis=0, keepdims=True)
+    cen_copy.wait()
+    chunk = 512
+
+    def gather(r, _):
+        number = labrow[r].astype(I32) - 1
+        total = jnp.zeros((depth, slots), F32)
+        for k in range(n_lists // chunk):
+            hot = (iota((chunk, slots), 0) == number - k * chunk).astype(BF16)
+            total = total + dot(cen_v[:, k * chunk:(k + 1) * chunk], hot)
+        cent[r] = total
+        return 0
+
+    lax.fori_loop(0, n_sub, gather, 0)
+
+    move_on(5)
     cb_copy.wait()
     log2e = math.log2(math.e)
     for g in range(groups):
@@ -205,72 +278,11 @@
         cbk[g] = jnp.swapaxes(stack, 0, 1).astype(BF16)
     acc[...] = jnp.zeros_like(acc)
 
-    most = labrecv.at[pl.ds(0, owners - 1)]
-    pltpu.make_async_copy(most, most, labr).wait()
-    lab = labrecv[...].reshape(owners, 128).astype(BF16)
-    for p, members in enumerate(parts):
-        each = len(members) * CAP
-        for b in range(len(members)):
-            lane = iota((128, slots), 1) + b * slots
-            want = lane % each + members[0] * CAP
-            q = iota((128, slots), 0)
-            pick = jnp.where(q == want, 64.0, jnp.where(q == want + 32, 1.0, 0.0)).astype(BF16)
-            from_j = (iota((owners, slots), 1) + b * slots) // each == iota((owners, slots), 0)
-            labrow[members[b]] = jnp.sum(jnp.where(from_j, dot(lab, pick), 0.0), axis=0, keepdims=True)
-    cen_copy.wait()
-    chunk = 512
-
-    def gather(r, _):
-        number = labrow[r].astype(I32) - 1
-        total = jnp.zeros((depth, slots), F32)
-        for k in range(n_lists // chunk):
-            hot = (iota((chunk, slots), 0) == number - k * chunk).astype(BF16)
-            total = total + dot(cen_v[:, k * chunk:(k + 1) * chunk], hot)
-        cent[r] = total
-        return 0
-
-    lax.fori_loop(0, n_sub, gather, 0)
-
-    row = iota((16, slots), 0)
-
-    def prepare(r):
-        present = (labrow[r] > 0.5).astype(F32)
-        arrived = recv[pl.ds(pl.multiple_of(r * slots, slots), slots)]
-        return present, jnp.swapaxes(arrived, 0, 1) - cent[r]
-
-    def sums(g, present, residual):
-        part = residual[g * width:(g + 1) * width]
-        r1, r2, r3 = split3(part)
-        ones = jnp.where(row < 3, 1.0, 0.0).astype(BF16)
-        fill = jnp.zeros((256 - 6 * width - 16, slots), BF16)
-        stack = jnp.concatenate([r1, r1, r1, r2, r2, r3, ones, fill], axis=0)
-        logits = dot(cbk[g], stack)
-        e = jnp.exp2(logits - jnp.max(logits, axis=0, keepdims=True))
-        inv = present / jnp.sum(e, axis=0, keepdims=True)
-        w = jnp.concatenate([part * inv, jnp.where(row == 0, inv, 0.0)], axis=0)
-        w = jnp.concatenate(split3(w), axis=0)
-        e1 = e.astype(BF16)
-        e2 = (e - e1.astype(F32)).astype(BF16)
-        return dot(w, e1, 1, 1) + dot(w, e2, 1, 1)
-
-    def work(r, _):
-        present, residual = prepare(r)
-        for g in range(groups):
-            acc[g] += sums(g, present, residual)
-        return 0
-
-    def arrival(p):
-        base, count = rows_of(p)
-        arrived = recv.at[pl.ds(base, count - len(parts[p]) * CAP)]
-        pltpu.make_async_copy(arrived, arrived, drecv.at[p]).wait()
-        own_part(p).wait()
-
-    for p, members in enumerate(parts[:-1]):
-        arrival(p)
-        if len(members) == 1:
-            work(members[0], 0)
-        else:
-            lax.fori_loop(members[0], members[-1] + 1, work, 0)
+    work_part(0)
+    work_part(1)
+    work_part(2)
+    work_part(3)
+    work_part(4)
 
     z, core = l // cores, lax.rem(l, cores)
     n_z, n_k = n_list // cores, n_slab * cores

time: 62.5 us -> 62.8 us (level)
  no operation moved by 1% of the time
where the time goes in v4:
time: 62.8 us; the launch traced here: 62.6 us
  Pallas kernels  62 us (99%)
  local copies, waits for them, and re-layouts  0.66 us (1%)
    pallas_call x1, Pallas kernels, per_device(): pl.pallas_call(functools.partial(kernel, dims), out_shape=pltpu.VMEM((gro...  62 us

profile of v4, /device:TPU:1, one launch (start us, length us, event | category | flops | bytes accessed | tf_op | source)
XLA Modules:
  0.0 62.6 jit_solution(18049421615687920682)
XLA Ops:
  0.0 62.0 %shard_map.46 = f32[4,32,256]{2,1,0:T(8,128)S(1)} custom-call(s32[1,128]{1,0:T(1,128)} %bitcast.5, f32[1024,128]{1,0:T(8,128)} %vec_ref.1, bf16[128,4096]{1,0:T(8,128)(2,1)} %cen_ref.1, f32[4,32,256]{2,1,0:T(8,128)} %bitcast.4), custom_call_target="tpu_custom_call" | custom-call | tf_op jit(solution)/shard_map/pallas_call | solution.py:373
  62.0 0.7 %copy.6 = f32[4,256,32]{1,2,0:T(8,128)} copy(f32[4,256,32]{1,2,0:T(8,128)S(1)} %bitcast.3) | data formatting | bytes 262144
